TPU v7x, 32 devices: a whole 2x2x4 slice. The times are simulated.
32 devices in a mesh: ctx: 8 (over z, y), head: 4 (over x, core).
Axes of the slice: x: 2, y: 2, z: 4, core: 2. Of those that a mesh axis runs over, the one named last changes fastest.
Arguments:
- queries: bfloat16 [2048, 2048], P('ctx', 'head'), may hold values from -6 to 6
- key_rows: bfloat16 [2048, 2048], P('ctx', 'head'), may hold values from -1.5 to 1.5
- value_rows: bfloat16 [2048, 2048], P('ctx', 'head'), may hold values from -6 to 6
- carry_state: float32 [16, 128, 128], P('head'), may hold values from -96 to 96
- decay_rate: float32 [16], P('head'), as said below
- norm_gain: float32 [2048], P('head'), may hold values from 0.5 to 1.5
- order: int32 [8, 256], P('ctx'), may hold values from 0 to 255, each once within a row
- doc_lengths: int32 [16], replicated, may hold values from 1 to 1024, 2048 in all
Outputs:
- mixed: bfloat16 [2048, 2048], P('ctx', 'head')
Inputs may be any that keep to these rules, and one draw needn't show every extreme that they name: `order`: each row is a permutation of 0..255. `doc_lengths`: they sum to 2048; the longest is exactly 1024. `decay_rate`: positive rates.
All inputs are finite; a program needn't handle non-finite values.
Results may differ from a plain program's by a relative error of at most 0.001.
Values may be sent and summed in bfloat16 or wider, within the bound.
A program may use at most 128 MiB of HBM per device.

v0:
```python
import jax
import jax.numpy as jnp
from jax import lax
from jax.sharding import PartitionSpec as P


def from_behind(value, axis, steps):
    count = lax.axis_size(axis)
    pairs = [(source, (source + steps) % count) for source in range(count)]
    return lax.ppermute(value, axis, pairs)


def entering(value, axis, combine, identity):
    peers, position = (lax.axis_size(axis), lax.axis_index(axis))
    everything = jax.tree.map(lambda part: lax.all_gather(part, axis), value)
    start = jax.tree.map(
        lambda part, zero: jnp.broadcast_to(jnp.asarray(zero, part.dtype), part.shape),
        value,
        identity,
    )

    def lap(k, before):
        reached = k < position
        new = combine(before, jax.tree.map(lambda part: part[k], everything))
        return jax.tree.map(lambda a, b: jnp.where(reached, a, b), new, before)

    return lax.fori_loop(0, peers, lap, start)


def shards(queries, key_rows, value_rows, carry_state, decay_rate, norm_gain, order, doc_lengths):
    row_count, feature_count = queries.shape
    head_count = decay_rate.shape[0]
    head_width = feature_count // head_count
    spill_count = row_count // 4
    block_size = min(512, row_count)
    highest = lax.Precision.HIGHEST
    permuted = order[0]
    kept_rows = permuted[: row_count - spill_count]
    moved_rows = permuted[row_count - spill_count :]
    outgoing = jnp.stack([queries[moved_rows], key_rows[moved_rows], value_rows[moved_rows]])
    arrived = from_behind(outgoing, "ctx", -1)
    ctx_query = jnp.concatenate([queries[kept_rows], arrived[0]], axis=0)
    ctx_key = jnp.concatenate([key_rows[kept_rows], arrived[1]], axis=0)
    ctx_value = jnp.concatenate([value_rows[kept_rows], arrived[2]], axis=0)
    device = lax.axis_index("ctx")
    offset_base = device * row_count
    doc_ends = jnp.cumsum(doc_lengths)

    def count_before(position):
        return jnp.sum((doc_ends <= position).astype(jnp.int32))

    positions = offset_base + jnp.arange(row_count, dtype=jnp.int32)
    segment = jnp.sum((doc_ends[None, :] <= positions[:, None]).astype(jnp.int32), axis=1)
    prior_device = count_before(offset_base - 1)
    offsets = jnp.arange(block_size, dtype=jnp.int32)
    distance = offsets[:, None] - offsets[None, :]
    lower = distance >= 0
    decay = jnp.exp(-decay_rate[:, None, None] * jnp.maximum(distance, 0).astype(jnp.float32)[None])
    leading = jnp.exp(-decay_rate[None, :] * (offsets + 1).astype(jnp.float32)[:, None])
    trailing = jnp.exp(
        -decay_rate[None, :] * (block_size - 1 - offsets).astype(jnp.float32)[:, None]
    )
    whole_block = jnp.exp(-decay_rate * jnp.float32(block_size))
    running = jnp.zeros((head_count, head_width, head_width), jnp.float32)
    query_block = ctx_query.reshape(block_size, head_count, head_width)
    key_block = ctx_key.reshape(block_size, head_count, head_width)
    value_block = ctx_value.reshape(block_size, head_count, head_width)
    prior = count_before(offset_base + 0 - 1)
    same_doc = (segment[:, None] == segment[None, :]) & lower
    scores = jnp.einsum("thd,shd->hts", query_block, key_block, preferred_element_type=jnp.float32)
    weights = jnp.where(same_doc[None], scores * decay, jnp.float32(0.0))
    value_f = value_block.astype(jnp.float32)
    attn = jnp.einsum("hts,shd->thd", weights, value_f, precision=highest)
    carry_on = (segment == prior).astype(jnp.float32)
    inter = jnp.einsum("thd,hde->the", query_block.astype(jnp.float32), running, precision=highest)
    attn = attn + inter * (leading * carry_on[:, None])[:, :, None]
    at_end = (segment == segment[-1]).astype(jnp.float32)
    scaled_keys = key_block.astype(jnp.float32) * (trailing * at_end[:, None])[:, :, None]
    added = jnp.einsum("shd,she->hde", scaled_keys, value_f, precision=highest)
    keep_factor = jnp.where(segment[-1] == prior, whole_block, jnp.float32(0.0))
    running = keep_factor[:, None, None] * running + added
    local_attn = attn
    reach = jnp.where(
        segment[-1] == prior_device, jnp.exp(-decay_rate * jnp.float32(row_count)), jnp.float32(0.0)
    )
    initial = carry_state * (device == 0).astype(jnp.float32)
    element = reach[:, None, None] * initial + running

    def combine(earlier, latter):
        return (earlier[0] * latter[0], latter[0][:, None, None] * earlier[1] + latter[1])

    identity = (jnp.ones_like(reach), jnp.zeros_like(element))
    incoming = entering((reach, element), "ctx", combine, identity)[1]
    incoming = incoming + initial
    device_on = (segment == prior_device).astype(jnp.float32)
    local_offsets = jnp.arange(row_count, dtype=jnp.int32)
    lead_all = (
        jnp.exp(-decay_rate[None, :] * (local_offsets + 1).astype(jnp.float32)[:, None])
        * device_on[:, None]
    )
    query_all = ctx_query.reshape(row_count, head_count, head_width).astype(jnp.float32)
    carried = jnp.einsum("thd,hde->the", query_all, incoming, precision=highest)
    local_attn = local_attn + carried * lead_all[:, :, None]
    flat = local_attn.reshape(row_count, feature_count)
    square_total = lax.psum(jnp.sum(flat * flat, axis=1), "head")
    mean_sq = square_total / jnp.float32(feature_count * lax.axis_size("head"))
    normed = (flat * lax.rsqrt(mean_sq + 1e-05)[:, None] * norm_gain[None, :]).astype(jnp.bfloat16)
    returned = from_behind(normed[row_count - spill_count :], "ctx", 1)
    result = jnp.zeros_like(queries).at[kept_rows].set(normed[: row_count - spill_count])
    return result.at[moved_rows].set(returned)


def solution(mesh):
    return jax.shard_map(
        shards,
        mesh=mesh,
        in_specs=(
            P("ctx", "head"),
            P("ctx", "head"),
            P("ctx", "head"),
            P("head", None, None),
            P("head"),
            P("head"),
            P("ctx", None),
            P(),
        ),
        out_specs=P("ctx", "head"),
        check_vma=False,
    )
```

profile of v0, /device:TPU:0, one launch (start us, length us, event | category | flops | bytes accessed | tf_op | source)
XLA Modules:
  0.0 108.1 jit_solution(18076214734327120386)
XLA Ops:
  6.5 0.7 compare_select_fusion
  7.3 0.7 fusion.20
  8.0 1.7 %gather_fusion.1 = bf16[64,512]{1,0:T(8,128)(2,1)S(1)} fusion(bf16[256,512]{1,0:T(8,128)(2,1)} %param.10, s32[1024]{0:T(1024)S(1)} %get-tuple-element.140), kind=kCustom, calls=%fused_computation.1 | custom fusion | bytes 131328 | tf_op jit(solution)/shard_map/gather | solution.py:40
  9.7 0.7 gather_fusion.2
  10.4 1.7 %gather_fusion.3 = bf16[64,512]{1,0:T(8,128)(2,1)S(1)} fusion(bf16[256,512]{1,0:T(8,128)(2,1)} %param.12, s32[1024]{0:T(1024)S(1)} %get-tuple-element.140), kind=kCustom, calls=%fused_computation.3 | custom fusion | bytes 131328 | tf_op jit(solution)/shard_map/gather | solution.py:40
  12.2 6.1 %collective-permute-start = (bf16[3,64,512]{2,1,0:T(8,128)(2,1)S(1)}, bf16[3,64,512]{2,1,0:T(8,128)(2,1)S(1)}, u32[]{:S(2)}, u32[]{:S(2)}) collective-permute-start(bf16[3,64,512]{2,1,0:T(8,128)(2,1)S(1)} %pad_maximum_fusion.1), channel_id=1, source_target_pairs={{0,28},{4,0},{8,4},{12,8},{16,12},{20,16},{24,20},{28,24},{1,29},{... | collective-permute-start | bytes 589832 | tf_op jit(solution)/shard_map/ppermute | solution.py:10
  19.2 0.7 fusion.19
  19.9 1.3 %compare_convert_fusion.1 = (f32[256]{0:T(256)S(1)}, f32[256]{0:T(256)S(1)}) fusion(s32[256]{0:T(256)S(1)} %convert_reduce_fusion, s32[]{:T(128)} %fusion.19, s32[]{:T(128)} %bitcast.12), kind=kLoop, calls=%fused_computation.52 | loop fusion | flops 1024 | bytes 3080 | tf_op jit(solution)/shard_map/convert_element_type | solution.py:74
  22.6 1.0 gather_fusion.5
  23.6 1.0 gather_fusion
  25.2 1.5 %fusion.6 = f32[4,128,128]{2,1,0:T(8,128)} fusion(bf16[256,4,128]{2,0,1:T(8,128)(2,1)S(1)} %copy_dynamic-update-slice_fusion, f32[256,4]{0,1:T(4,128)S(1)} %get-tuple-element.136, f32[4,128,128]{2,1,0:T(8,128)S(1)} %copy-done.3, f32[4]{0:T(128)S(1)} %get-tuple-element.128, f32[]{:T(128)S(6)} %convert_element_type.61, f32[4]{0:T(128)S(1)} %get-tuple-element.129, ...), kind=kOutput, calls=%fused_computation.21 | convolution fusion | flops 202375168 | bytes 1052708 | tf_op jit(solution)/shard_map/shd,she->hde/dot_general | solution.py:79
  26.7 1.0 gather_fusion.4
  27.7 0.6 dynamic-slice
  29.2 19.7 %all-reduce = f32[32]{0:T(128)S(1)} all-reduce(f32[32]{0:T(128)S(1)} %dynamic-update-slice), channel_id=2, replica_groups=mesh['ctx'=8,'head'=4] {'ctx'}, use_global_device_ids=true, to_apply=%add | all-reduce | flops 32 | bytes 256
  49.1 0.7 fusion.12
  50.3 1.2 %fusion.1 = f32[4,256,256]{2,1,0:T(8,128)S(1)} fusion(bf16[256,4,128]{2,0,1:T(8,128)(2,1)S(1)} %copy_dynamic-update-slice_fusion.1, bf16[256,4,128]{2,0,1:T(8,128)(2,1)S(1)} %copy_dynamic-update-slice_fusion, f32[256,256]{1,0:T(8,128)S(1)} %maximum_convert_fusion, f32[4]{0:T(128)S(1)} %get-tuple-element.137, pred[256,256]{1,0:T(8,128)(4,1)} %fusion.12), kind=kOutput, calls=%fused_computation.12 | convolution fusion | flops 67895296 | bytes 1900560 | tf_op jit(solution)/shard_map/thd,shd->hts/dot_general | solution.py:70
  51.4 24.3 %all-gather.4.cloned.1.call-done = f32[32,128,128]{2,1,0:T(8,128)} async-done(((f32[4,128,128]{2,1,0:T(8,128)}), f32[32,128,128]{2,1,0:T(8,128)}) %all-gather.4.cloned.1.call-update) | async-done | bytes 2097168 | tf_op jit(solution)/shard_map/all_gather | solution.py:15
  75.8 8.7 %while.14 = (s32[]{:T(128)}, f32[4,128,128]{2,1,0:T(8,128)S(1)}, s32[]{:T(128)}, f32[8,4]{1,0:T(8,128)S(1)}, f32[8,4,128,128]{3,2,1,0:T(8,128)}, /*index=5*/s32[]{:T(128)}, s32[]{:T(128)}) while((s32[]{:T(128)}, f32[4,128,128]{2,1,0:T(8,128)S(1)}, s32[]{:T(128)}, f32[8,4]{1,0:T(8,128)S(1)}, f32[8,4,128,128]{3,2,1,0:T(8,128)}, ...), condition=%wide.region_4.5_spmd.clone, body=%wide.region_3.4_spmd.clone.sunk | while | flops 262148 | bytes 786585 | solution.py:27
  75.8 1.0 fusion.33
  76.9 1.1 fusion.33
  78.0 1.1 fusion.33
  79.1 1.1 fusion.33
  80.1 1.1 fusion.33
  81.2 1.1 fusion.33
  82.3 1.1 fusion.33
  83.4 1.1 fusion.33
  84.9 0.8 multiply_reduce_fusion
  85.9 5.7 %psum.7 = f32[256]{0:T(256)S(1)} all-reduce(f32[256]{0:T(256)S(1)} %get-tuple-element.138), channel_id=1, replica_groups=mesh['ctx'=8,'head'=4] {'head'}, use_global_device_ids=true, to_apply=%region_6.7 | all-reduce | flops 256 | bytes 2048 | tf_op jit(solution)/shard_map/psum | solution.py:105
  91.7 0.6 collective-permute-start.1
  92.3 2.0 %scatter_custom_fusion = bf16[256,512]{1,0:T(8,128)(2,1)} fusion(s32[192]{0:T(256)S(1)} %bitcast.66, bf16[256,512]{1,0:T(8,128)(2,1)S(1)} %multiply_convert_fusion, bf16[]{:T(256)} %constant.47.clone.1), kind=kCustom, calls=%fused_computation.36 | custom fusion | bytes 458754 | tf_op jit(solution)/shard_map/scatter | solution.py:109
  94.3 4.5 %collective-permute-done.1 = bf16[64,512]{1,0:T(8,128)(2,1)S(1)} collective-permute-done((bf16[64,512]{1,0:T(8,128)(2,1)S(1)}, bf16[64,512]{1,0:T(8,128)(2,1)S(1)}, u32[]{:S(2)}, u32[]{:S(2)}) %collective-permute-start.1) | collective-permute-done | bytes 65568 | tf_op jit(solution)/shard_map/ppermute | solution.py:10
  98.8 2.5 %scatter_fusion = bf16[256,512]{1,0:T(8,128)(2,1)} fusion(bf16[256,512]{1,0:T(8,128)(2,1)} %scatter_custom_fusion, s32[64]{0:T(128)S(1)} %copy-done.6, bf16[64,512]{1,0:T(8,128)(2,1)S(1)} %collective-permute-done.1), kind=kCustom, calls=%fused_computation.7 | custom fusion | bytes 196864 | tf_op jit(solution)/shard_map/scatter | solution.py:110
  (62 shorter events, 3.1 us)
Async XLA Ops:
  6.5 3.2 %copy-start = (bf16[256,512]{1,0:T(8,128)(2,1)S(1)}, bf16[256,512]{1,0:T(8,128)(2,1)}, u32[]{:S(2)}) copy-start(bf16[256,512]{1,0:T(8,128)(2,1)} %param.11) | copy-start | bytes 786436
  6.5 17.1 %copy-start.1 = (bf16[256,512]{1,0:T(8,128)(2,1)S(1)}, bf16[256,512]{1,0:T(8,128)(2,1)}, u32[]{:S(2)}) copy-start(bf16[256,512]{1,0:T(8,128)(2,1)} %param.12) | copy-start | bytes 786436
  6.5 11.7 %copy-start.7 = (s32[16]{0:T(128)S(1)}, s32[16]{0:T(128)}, u32[]{:S(2)}) copy-start(s32[16]{0:T(128)} %param.17) | copy-start | bytes 196
  6.5 69.2 %all-gather.4.cloned.1.call-start = ((), (), s32[]{:S(2)}) async-start(), calls=%async_computation | async-start | bytes 2359296 | tf_op jit(solution)/shard_map/all_gather | solution.py:15
  8.0 14.5 %copy-start.5 = (s32[64]{0:T(128)}, s32[64]{0:T(128)S(1)}, u32[]{:S(2)}) copy-start(s32[64]{0:T(128)S(1)} %fusion.20) | copy-start | bytes 772
  12.2 12.8 %collective-permute-start = (bf16[3,64,512]{2,1,0:T(8,128)(2,1)S(1)}, bf16[3,64,512]{2,1,0:T(8,128)(2,1)S(1)}, u32[]{:S(2)}, u32[]{:S(2)}) collective-permute-start(bf16[3,64,512]{2,1,0:T(8,128)(2,1)S(1)} %pad_maximum_fusion.1), channel_id=1, source_target_pairs={{0,28},{4,0},{8,4},{12,8},{16,12},{20,16},{24,20},{28,24},{1,29},{... | collective-permute-start | bytes 589832 | tf_op jit(solution)/shard_map/ppermute | solution.py:10
  22.6 2.3 %copy-start.8 = (f32[4]{0:T(128)S(1)}, f32[4]{0:T(128)}, u32[]{:S(2)}) copy-start(f32[4]{0:T(128)} %param.14) | copy-start | bytes 52
  23.6 1.5 %copy-start.3 = (f32[4,128,128]{2,1,0:T(8,128)S(1)}, f32[4,128,128]{2,1,0:T(8,128)}, u32[]{:S(2)}) copy-start(f32[4,128,128]{2,1,0:T(8,128)} %param.13) | copy-start | bytes 786436
  23.6 3.1 %copy-start.2 = (bf16[256,512]{1,0:T(8,128)(2,1)S(1)}, bf16[256,512]{1,0:T(8,128)(2,1)}, u32[]{:S(2)}) copy-start(bf16[256,512]{1,0:T(8,128)(2,1)} %param.10) | copy-start | bytes 786436
  24.8 2.9 %copy-start.9 = (u32[32]{0:T(128)S(1)}, u32[32]{0:T(128)}, u32[]{:S(2)}) copy-start(u32[32]{0:T(128)} %constant.62) | copy-start | bytes 388
  84.9 6.7 %copy-start.4 = (f32[512]{0:T(512)S(1)}, f32[512]{0:T(512)}, u32[]{:S(2)}) copy-start(f32[512]{0:T(512)} %param.15) | copy-start | bytes 6148
  84.9 13.8 %copy-start.6 = (s32[64]{0:T(128)S(1)}, s32[64]{0:T(128)}, u32[]{:S(2)}) copy-start(s32[64]{0:T(128)} %copy-done.5) | copy-start | bytes 772
  91.7 7.0 %collective-permute-start.1 = (bf16[64,512]{1,0:T(8,128)(2,1)S(1)}, bf16[64,512]{1,0:T(8,128)(2,1)S(1)}, u32[]{:S(2)}, u32[]{:S(2)}) collective-permute-start(bf16[64,512]{1,0:T(8,128)(2,1)S(1)} %slice.58), channel_id=1, source_target_pairs={{0,4},{4,8},{8,12},{12,16},{16,20},{20,24},{24,28},{28,0},{1,5},{5... | collective-permute-start | bytes 196616 | tf_op jit(solution)/shard_map/ppermute | solution.py:10
Sparse Core Ops, SparseCore 0:
  26.8 48.9 all-gather.3
where the time goes:
time: 109 us; the launch traced here: 108 us
  waiting for transfers between devices  28.8 us (26%)
  blocking collectives  25.4 us (23%)
  between operations  15.7 us (14%)
  local copies, waits for them, and re-layouts  13.9 us (13%)
  other arithmetic  13.2 us (12%)
  starting transfers between devices  6.66 us (6%)
  matrix products  4.25 us (4%)
    all_gather x1, waiting for transfers between devices, entering(): everything = jax.tree.map(lambda part: lax.all_gather(part, axis), value)  24.3 us
    unnamed x1, blocking collectives  19.7 us
    select_n x8, other arithmetic, lap(): return jax.tree.map(lambda a, b: jnp.where(reached, a, b), new, before)  8.42 us
    ppermute x2, starting transfers between devices, from_behind(): return lax.ppermute(value, axis, pairs)  6.66 us
    psum x1, blocking collectives, shards(): square_total = lax.psum(jnp.sum(flat * flat, axis=1), 'head')  5.67 us
    ppermute x2, waiting for transfers between devices, from_behind(): return lax.ppermute(value, axis, pairs)  4.46 us
    scatter x1, local copies, waits for them, and re-layouts, shards(): return result.at[moved_rows].set(returned)  2.47 us
  transfers between devices with their start and end apart: 3, of which 2 were waited for; matrix products, arithmetic and copies ran while one was open for 11% of the time, Pallas kernels for 0%

commit v1 on v0

v1 whole, which is shorter than its diff:
```python
import functools

import jax
import jax.numpy as jnp
from jax import lax
from jax.experimental import pallas as pl
from jax.experimental.pallas import tpu as pltpu
from jax.sharding import PartitionSpec as P

F32 = jnp.float32
BF16 = jnp.bfloat16
MESH = pl.DeviceIdType.MESH


def split(x):
    high = x.astype(BF16)
    return high, (x - high.astype(F32)).astype(BF16)


def dot(a, b, contract):
    return lax.dot_general(a, b, ((contract[:1], contract[1:]), ((), ())), preferred_element_type=F32)


def two_term(a, b, contract):
    width = b.shape[1]
    both = dot(a, jnp.concatenate(split(b), axis=1), contract)
    return both[:, :width] + both[:, width:]


def kernel(
    n_ctx, n_head, reach,
    rate_ref, docs_ref, q_ref, k_ref, v_ref, carry_ref, gain_ref, order_ref, out_ref,
    attn, pair, away, layer, landed, onward, arrived, squares, squares_in,
    pair_send, pair_recv, layer_send, layer_recv, onward_send, onward_recv, sq_send, sq_recv,
):
    rows, features = q_ref.shape
    heads = rate_ref.shape[0]
    width = features // heads
    half = heads // 2
    n_docs = docs_ref.shape[0]
    spill = rows // 4
    keep = rows - spill
    tokens = n_ctx * rows
    n_pairs = n_ctx // 2
    d = lax.axis_index("ctx")
    g = lax.axis_index("head")
    u = d // 2
    y = lax.rem(d, 2)
    partner = d + 1 - 2 * y
    mine = y * half
    other = (1 - y) * half

    def sends(b):
        return u + b <= n_pairs

    def receives(b):
        return (u >= b) | (u == 0)

    barrier = pltpu.get_barrier_semaphore()
    pl.semaphore_signal(barrier, inc=1, device_id=(partner, g), device_id_type=MESH)
    for j in range(1, n_head):
        pl.semaphore_signal(
            barrier, inc=1, device_id=(d, lax.rem(g + n_head - j, n_head)), device_id_type=MESH
        )
    expected = jnp.int32(n_head)
    for b in range(1, reach + 1):
        @pl.when(receives(b))
        def _():
            source = lax.rem(u + n_pairs - b, n_pairs) * 2 + y
            pl.semaphore_signal(barrier, inc=1, device_id=(source, g), device_id_type=MESH)
        expected = expected + sends(b).astype(jnp.int32)

    base = jnp.where(d == 0, tokens, d * rows) - spill
    last = d * rows + keep - 1
    chosen = (order_ref[...] == lax.broadcasted_iota(jnp.int32, (rows, rows), 0)).astype(F32).astype(BF16)
    index = lax.broadcasted_iota(jnp.int32, (rows, rows), 0).astype(F32).astype(BF16)
    along = lax.broadcasted_iota(jnp.int32, (16, rows), 1).astype(F32).astype(BF16)

    def position(slot):
        kept_at = (d * rows).astype(F32)
        moved_at = (base - keep).astype(F32)
        return slot + jnp.where(slot < keep, kept_at, moved_at)

    down = position(dot(chosen, index, (1, 0)))
    across = position(dot(along, chosen, (1, 1)))[0:1]
    pos = down[:, :width]

    pair_last = 2 * u * rows + rows + keep - 1
    first_last = 2 * u * rows + keep - 1
    pair_base = jnp.where(u == 0, tokens, 2 * u * rows) - spill
    marks = (last, pair_last, first_last, pair_base - 1)

    def document(n, carried):
        edge, begin, scalars = carried
        edge = edge + docs_ref[n]
        mark = edge.astype(F32)
        begin = jnp.where(pos >= mark, mark, begin)
        return edge, begin, tuple(jnp.where(m >= edge, edge, s) for m, s in zip(marks, scalars))

    zero = jnp.int32(0)
    state = (zero, jnp.zeros((rows, width), F32), (zero,) * 4)
    if n_docs <= 32:
        for n in range(n_docs):
            state = document(n, state)
    else:
        state = lax.fori_loop(0, n_docs, document, state)
    _, begin, (last_begin, pair_begin, first_begin, base_begin) = state

    inf = jnp.float32(jnp.inf)

    def decay(h, steps):
        return jnp.exp(-rate_ref[h] * steps)

    def factor(h, steps, holds):
        return decay(h, jnp.full((1, width), jnp.where(holds, jnp.float32(steps), inf)))

    def columns(ref, h):
        return ref[:, pl.ds(pl.multiple_of(h * width, width), width)]

    to_last = jnp.where((pos <= last.astype(F32)) & (pos >= last_begin.astype(F32)), last.astype(F32) - pos, inf)

    def own_state(h):
        weighted = columns(v_ref, h).astype(F32) * decay(h, to_last)
        return two_term(columns(k_ref, h), weighted, (0, 0))

    def copy(src, dst, send, recv, target):
        return pltpu.make_async_remote_copy(
            src_ref=src, dst_ref=dst, send_sem=send, recv_sem=recv, device_id=target, device_id_type=MESH
        )

    pair_copies = []
    for i in range(half):
        away[i] = own_state(other + i)
        if i == 0:
            pl.semaphore_wait(barrier, expected)
        c = copy(away.at[i], pair.at[y, i], pair_send.at[i], pair_recv.at[i], (partner, g))
        c.start()
        pair_copies.append(c)
    for i in range(half):
        pair[y, i] = own_state(mine + i)

    def layer_copy(b, i):
        target = lax.rem(u + b, n_pairs) * 2 + y
        return copy(layer.at[i], landed.at[b - 1, i], layer_send.at[b - 1, i], layer_recv.at[b - 1, i], (target, g))

    for i in range(half):
        pair_copies[i].wait_recv()
        layer[i] = pair[1, i] + factor(mine + i, rows, pair_begin <= pair_last - rows) * pair[0, i]
        for b in range(1, reach + 1):
            @pl.when(sends(b))
            def _():
                layer_copy(b, i).start()

    gap = down - across
    begins = jnp.concatenate([begin] * (rows // width), axis=1)
    gap = jnp.where((gap >= 0) & (across >= begins), gap, inf)
    to_carry = jnp.where(begin == 0, pos + 1, inf)
    for h in range(heads):
        cols = slice(h * width, (h + 1) * width)
        q, v = q_ref[:, cols], v_ref[:, cols]
        weights = dot(q, k_ref[:, cols], (1, 1)) * decay(h, gap)
        high, low = split(weights)
        local = dot(high, v, (1, 0)) + dot(low, v, (1, 0))
        attn[:, cols] = local + two_term(q, carry_ref[h], (1, 0)) * decay(h, to_carry)

    to_base = jnp.where(
        (pos >= base.astype(F32)) & (begin < base.astype(F32)), pos - (base - 1).astype(F32), inf
    )

    def add_incoming(h, incoming):
        entering = two_term(columns(q_ref, h), incoming, (1, 0)) * decay(h, to_base)
        total = columns(attn, h) + entering
        attn[:, pl.ds(pl.multiple_of(h * width, width), width)] = total
        return total * total

    onward_copies = []
    kept = []
    for i in range(half):
        h = mine + i
        onward[i] = jnp.zeros((width, width), F32)
        for b in range(1, reach + 1):
            @pl.when(receives(b))
            def _():
                layer_copy(b, i).wait_recv()
                steps = 2 * rows * (b - 1)
                onward[i] += factor(h, steps, base_begin <= pair_base - 1 - steps) * landed[b - 1, i]
        before_first = onward[i]
        before_second = pair[0, i] + factor(h, rows, first_begin <= first_last - rows) * before_first
        is_first = y == 0
        onward[i] = jnp.where(is_first, before_second, before_first)
        c = copy(onward.at[i], arrived.at[i], onward_send.at[i], onward_recv.at[i], (partner, g))
        c.start()
        onward_copies.append(c)
        kept.append(jnp.where(is_first, before_first, before_second))
    power = jnp.zeros((rows, width), F32)
    for i in range(half):
        power += add_incoming(mine + i, kept[i])
    for i in range(half):
        onward_copies[i].wait_recv()
        power += add_incoming(other + i, arrived[i])

    ones = jnp.ones((16, width), BF16)
    high, low = split(power)
    squares[...] = (dot(ones, high, (1, 1)) + dot(ones, low, (1, 1)))[:8]
    sq_copies = []
    for j in range(1, n_head):
        c = copy(
            squares, squares_in.at[j - 1], sq_send.at[j - 1], sq_recv.at[j - 1], (d, lax.rem(g + j, n_head))
        )
        c.start()
        sq_copies.append(c)
    total = squares[...]
    for j in range(1, n_head):
        sq_copies[j - 1].wait_recv()
        total = total + squares_in[j - 1]
    scale = lax.rsqrt(total / jnp.float32(features * n_head) + 1e-5)
    scale = jnp.broadcast_to(scale[0:1], (width, rows)).T
    for h in range(heads):
        cols = slice(h * width, (h + 1) * width)
        out_ref[:, cols] = (attn[:, cols] * scale * gain_ref[:, cols]).astype(BF16)

    for c in pair_copies + onward_copies + sq_copies:
        c.wait_send()
    for i in range(half):
        for b in range(1, reach + 1):
            @pl.when(sends(b))
            def _():
                layer_copy(b, i).wait_send()


def shards(queries, key_rows, value_rows, carry_state, decay_rate, norm_gain, order, doc_lengths):
    rows, features = queries.shape
    heads, width, _ = carry_state.shape
    n_ctx, n_head = lax.axis_size("ctx"), lax.axis_size("head")
    longest = min(n_ctx * rows // 2, 2048)
    reach = -(-longest // (2 * rows))
    half = heads // 2
    vmem = pl.BlockSpec(memory_space=pltpu.VMEM)
    smem = pl.BlockSpec(memory_space=pltpu.SMEM)
    dma = pltpu.SemaphoreType.DMA
    return pl.pallas_call(
        functools.partial(kernel, n_ctx, n_head, reach),
        out_shape=jax.ShapeDtypeStruct((rows, features), BF16),
        in_specs=[smem, smem] + [vmem] * 6,
        out_specs=vmem,
        scratch_shapes=[
            pltpu.VMEM((rows, features), F32),
            pltpu.VMEM((2, half, width, width), F32),
            pltpu.VMEM((half, width, width), F32),
            pltpu.VMEM((half, width, width), F32),
            pltpu.VMEM((reach, half, width, width), F32),
            pltpu.VMEM((half, width, width), F32),
            pltpu.VMEM((half, width, width), F32),
            pltpu.VMEM((8, rows), F32),
            pltpu.VMEM((n_head - 1, 8, rows), F32),
            dma((half,)), dma((half,)),
            dma((reach, half)), dma((reach, half)),
            dma((half,)), dma((half,)),
            dma((n_head - 1,)), dma((n_head - 1,)),
        ],
        compiler_params=pltpu.CompilerParams(
            collective_id=0, has_side_effects=True, vmem_limit_bytes=32 * 1024 * 1024
        ),
    )(decay_rate, doc_lengths, queries, key_rows, value_rows, carry_state, norm_gain.reshape(1, features), order)


def solution(mesh):
    return jax.shard_map(
        shards,
        mesh=mesh,
        in_specs=(
            P("ctx", "head"),
            P("ctx", "head"),
            P("ctx", "head"),
            P("head", None, None),
            P("head"),
            P("head"),
            P("ctx", None),
            P(),
        ),
        out_specs=P("ctx", "head"),
        check_vma=False,
    )
```

time: 109 us -> 29 us (0.27)
  waiting for transfers between devices: 28.8 us -> 0 us
  blocking collectives: 25.4 us -> 0 us
  Pallas kernels: 0 us -> 21.9 us
  between operations: 15.7 us -> 0.02 us
  other arithmetic: 13.2 us -> 0 us
  local copies, waits for them, and re-layouts: 13.9 us -> 6.52 us
  starting transfers between devices: 6.66 us -> 0 us
  matrix products: 4.25 us -> 0 us
    all_gather x1 -> x0, waiting for transfers between devices: 24.3 us -> none  [entering(): everything = jax.tree.map(lambda part: lax.all_gather(part, axis), value)]
    pallas_call x0 -> x1, Pallas kernels: none -> 21.9 us  [shards(): pl.pallas_call(functools.partial(kernel, n_ctx, n_head, reach), out_shape...]
    unnamed x1 -> x0, blocking collectives: 19.7 us -> none
    select_n x10 -> x0, other arithmetic: 9.89 us -> none  [the longest x8 8.42 us: lap(): return jax.tree.map(lambda a, b: jnp.where(reached, a, b), new, before)]
    gather x7 -> x0, local copies, waits for them, and re-layouts: 7.24 us -> none  [the longest x1 1.7 us: shards(): queries[moved_rows]]
    ppermute x2 -> x0, starting transfers between devices: 6.66 us -> none  [from_behind(): return lax.ppermute(value, axis, pairs)]
    psum x1 -> x0, blocking collectives: 5.67 us -> none  [shards(): square_total = lax.psum(jnp.sum(flat * flat, axis=1), 'head')]
    unnamed x25 -> x17, local copies, waits for them, and re-layouts: 0.96 us -> 6.52 us
  transfers between devices with their start and end apart: 3 -> 0, of which waited for: 2 -> 0; matrix products, arithmetic and copies ran while one was open for 11% -> 0% of each run, Pallas kernels for 0% -> 0%
where the time goes in v1:
time: 29 us; the launch traced here: 28.5 us
  Pallas kernels  21.9 us (76%)
  local copies, waits for them, and re-layouts  6.52 us (22%)
    pallas_call x1, Pallas kernels, shards(): pl.pallas_call(functools.partial(kernel, n_ctx, n_head, reach), out_shape...  21.9 us
    unnamed x17, local copies, waits for them, and re-layouts  6.52 us

profile of v1, /device:TPU:0, one launch (start us, length us, event | category | flops | bytes accessed | tf_op | source)
XLA Modules:
  0.0 28.5 jit_solution(17724262112322846319)
XLA Ops:
  0.0 0.0 copy-start.5
  0.0 0.0 copy-start.6
  0.0 0.7 %copy-done.5 = s32[1,256]{1,0:T(1,128)S(1)} copy-done((s32[1,256]{1,0:T(1,128)S(1)}, s32[1,256]{1,0:T(1,128)}, u32[]{:S(2)}) %copy-start.5) | copy-done | bytes 1048
  0.7 0.0 copy-done.6
  0.7 0.0 copy-start
  0.7 0.9 %copy-done = bf16[256,512]{1,0:T(8,128)(2,1)S(1)} copy-done((bf16[256,512]{1,0:T(8,128)(2,1)S(1)}, bf16[256,512]{1,0:T(8,128)(2,1)}, u32[]{:S(2)}) %copy-start) | copy-done | bytes 262168
  1.6 0.0 copy-start.1
  1.6 0.9 %copy-done.1 = bf16[256,512]{1,0:T(8,128)(2,1)S(1)} copy-done((bf16[256,512]{1,0:T(8,128)(2,1)S(1)}, bf16[256,512]{1,0:T(8,128)(2,1)}, u32[]{:S(2)}) %copy-start.1) | copy-done | bytes 262168
  2.6 0.0 copy-start.2
  2.6 0.9 %copy-done.2 = bf16[256,512]{1,0:T(8,128)(2,1)S(1)} copy-done((bf16[256,512]{1,0:T(8,128)(2,1)S(1)}, bf16[256,512]{1,0:T(8,128)(2,1)}, u32[]{:S(2)}) %copy-start.2) | copy-done | bytes 262168
  3.5 0.0 copy-start.3
  3.5 0.9 %copy-done.3 = f32[4,128,128]{2,1,0:T(8,128)S(1)} copy-done((f32[4,128,128]{2,1,0:T(8,128)S(1)}, f32[4,128,128]{2,1,0:T(8,128)}, u32[]{:S(2)}) %copy-start.3) | copy-done | bytes 262168
  4.5 0.0 copy-start.4
  4.5 0.7 %copy-done.4 = f32[512]{0:T(512)S(1)} copy-done((f32[512]{0:T(512)S(1)}, f32[512]{0:T(512)}, u32[]{:S(2)}) %copy-start.4) | copy-done | bytes 2072
  5.2 0.0 copy-start.7
  5.2 0.7 %copy-done.7 = s32[16]{0:T(128)S(1)} copy-done((s32[16]{0:T(128)S(1)}, s32[16]{0:T(128)}, u32[]{:S(2)}) %copy-start.7) | copy-done | bytes 88
  5.8 21.9 %shard_map.82 = bf16[256,512]{1,0:T(8,128)(2,1)S(1)} custom-call(f32[4]{0:T(128)S(1)} %copy-done.6, s32[16]{0:T(128)S(1)} %copy-done.7, bf16[256,512]{1,0:T(8,128)(2,1)S(1)} %copy-done, bf16[256,512]{1,0:T(8,128)(2,1)S(1)} %copy-done.1, bf16[256,512]{1,0:T(8,128)(2,1)S(1)} %copy-done.2, f32[4,128,128]{2,1,0:T(8,128)S(1)} %copy-done.3, f32[1,512]{1,0:T(1,128)S(1)} %bitcast.1, ...), custom_call_target="tpu_custom_call" | custom-call | tf_op jit(solution)/shard_map/pallas_call | solution.py:241
  27.8 0.7 %copy.10 = bf16[256,512]{1,0:T(8,128)(2,1)} copy(bf16[256,512]{1,0:T(8,128)(2,1)S(1)} %shard_map.82) | data formatting | bytes 524288
Async XLA Ops:
  0.0 0.7 %copy-start.5 = (s32[1,256]{1,0:T(1,128)S(1)}, s32[1,256]{1,0:T(1,128)}, u32[]{:S(2)}) copy-start(s32[1,256]{1,0:T(1,128)} %order_ref.1) | copy-start | bytes 3076
  0.0 0.7 %copy-start.6 = (f32[4]{0:T(128)S(1)}, f32[4]{0:T(128)}, u32[]{:S(2)}) copy-start(f32[4]{0:T(128)} %rate_ref.1) | copy-start | bytes 52
  0.7 1.0 %copy-start = (bf16[256,512]{1,0:T(8,128)(2,1)S(1)}, bf16[256,512]{1,0:T(8,128)(2,1)}, u32[]{:S(2)}) copy-start(bf16[256,512]{1,0:T(8,128)(2,1)} %q_ref.1) | copy-start | bytes 786436
  1.6 0.9 %copy-start.1 = (bf16[256,512]{1,0:T(8,128)(2,1)S(1)}, bf16[256,512]{1,0:T(8,128)(2,1)}, u32[]{:S(2)}) copy-start(bf16[256,512]{1,0:T(8,128)(2,1)} %k_ref.1) | copy-start | bytes 786436
  2.6 0.9 %copy-start.2 = (bf16[256,512]{1,0:T(8,128)(2,1)S(1)}, bf16[256,512]{1,0:T(8,128)(2,1)}, u32[]{:S(2)}) copy-start(bf16[256,512]{1,0:T(8,128)(2,1)} %v_ref.1) | copy-start | bytes 786436
  3.5 0.9 %copy-start.3 = (f32[4,128,128]{2,1,0:T(8,128)S(1)}, f32[4,128,128]{2,1,0:T(8,128)}, u32[]{:S(2)}) copy-start(f32[4,128,128]{2,1,0:T(8,128)} %carry_ref.1) | copy-start | bytes 786436
  4.5 0.7 %copy-start.4 = (f32[512]{0:T(512)S(1)}, f32[512]{0:T(512)}, u32[]{:S(2)}) copy-start(f32[512]{0:T(512)} %param.13) | copy-start | bytes 6148
  5.2 0.7 %copy-start.7 = (s32[16]{0:T(128)S(1)}, s32[16]{0:T(128)}, u32[]{:S(2)}) copy-start(s32[16]{0:T(128)} %docs_ref.1) | copy-start | bytes 196

commit v2 on v1

--- a/solution.py
+++ b/solution.py
@@ -29,7 +29,8 @@
 
 def kernel(
     n_ctx, n_head, reach,
-    rate_ref, docs_ref, q_ref, k_ref, v_ref, carry_ref, gain_ref, order_ref, out_ref,
+    rate_hbm, docs_hbm, q_hbm, k_hbm, v_hbm, carry_hbm, gain_hbm, order_hbm, out_ref,
+    rate_ref, docs_ref, q_ref, k_ref, v_ref, carry_ref, gain_ref, order_ref, load_sem,
     attn, pair, away, layer, landed, onward, arrived, squares, squares_in,
     pair_send, pair_recv, layer_send, layer_recv, onward_send, onward_recv, sq_send, sq_recv,
 ):
@@ -56,6 +57,15 @@
     def receives(b):
         return (u >= b) | (u == 0)
 
+    loads = {}
+    operands = (
+        (order_hbm, order_ref), (docs_hbm, docs_ref), (rate_hbm, rate_ref), (v_hbm, v_ref),
+        (k_hbm, k_ref), (q_hbm, q_ref), (carry_hbm, carry_ref), (gain_hbm, gain_ref),
+    )
+    for n, (source, held) in enumerate(operands):
+        loads[id(held)] = pltpu.make_async_copy(source, held, load_sem.at[n])
+        loads[id(held)].start()
+
     barrier = pltpu.get_barrier_semaphore()
     pl.semaphore_signal(barrier, inc=1, device_id=(partner, g), device_id_type=MESH)
     for j in range(1, n_head):
@@ -70,6 +80,9 @@
             pl.semaphore_signal(barrier, inc=1, device_id=(source, g), device_id_type=MESH)
         expected = expected + sends(b).astype(jnp.int32)
 
+    for held in (order_ref, docs_ref, rate_ref):
+        loads[id(held)].wait()
+
     base = jnp.where(d == 0, tokens, d * rows) - spill
     last = d * rows + keep - 1
     chosen = (order_ref[...] == lax.broadcasted_iota(jnp.int32, (rows, rows), 0)).astype(F32).astype(BF16)
@@ -128,6 +141,9 @@
             src_ref=src, dst_ref=dst, send_sem=send, recv_sem=recv, device_id=target, device_id_type=MESH
         )
 
+    loads[id(v_ref)].wait()
+    loads[id(k_ref)].wait()
+
     pair_copies = []
     for i in range(half):
         away[i] = own_state(other + i)
@@ -155,6 +171,8 @@
     begins = jnp.concatenate([begin] * (rows // width), axis=1)
     gap = jnp.where((gap >= 0) & (across >= begins), gap, inf)
     to_carry = jnp.where(begin == 0, pos + 1, inf)
+    loads[id(q_ref)].wait()
+    loads[id(carry_ref)].wait()
     for h in range(heads):
         cols = slice(h * width, (h + 1) * width)
         q, v = q_ref[:, cols], v_ref[:, cols]
@@ -215,6 +233,7 @@
         total = total + squares_in[j - 1]
     scale = lax.rsqrt(total / jnp.float32(features * n_head) + 1e-5)
     scale = jnp.broadcast_to(scale[0:1], (width, rows)).T
+    loads[id(gain_ref)].wait()
     for h in range(heads):
         cols = slice(h * width, (h + 1) * width)
         out_ref[:, cols] = (attn[:, cols] * scale * gain_ref[:, cols]).astype(BF16)
@@ -236,14 +255,23 @@
     reach = -(-longest // (2 * rows))
     half = heads // 2
     vmem = pl.BlockSpec(memory_space=pltpu.VMEM)
-    smem = pl.BlockSpec(memory_space=pltpu.SMEM)
+    hbm = pl.BlockSpec(memory_space=pltpu.HBM)
     dma = pltpu.SemaphoreType.DMA
     return pl.pallas_call(
         functools.partial(kernel, n_ctx, n_head, reach),
         out_shape=jax.ShapeDtypeStruct((rows, features), BF16),
-        in_specs=[smem, smem] + [vmem] * 6,
+        in_specs=[hbm] * 8,
         out_specs=vmem,
         scratch_shapes=[
+            pltpu.SMEM(decay_rate.shape, F32),
+            pltpu.SMEM(doc_lengths.shape, jnp.int32),
+            pltpu.VMEM((rows, features), BF16),
+            pltpu.VMEM((rows, features), BF16),
+            pltpu.VMEM((rows, features), BF16),
+            pltpu.VMEM(carry_state.shape, F32),
+            pltpu.VMEM((1, features), F32),
+            pltpu.VMEM(order.shape, jnp.int32),
+            dma((8,)),
             pltpu.VMEM((rows, features), F32),
             pltpu.VMEM((2, half, width, width), F32),
             pltpu.VMEM((half, width, width), F32),
@@ -259,7 +287,7 @@
             dma((n_head - 1,)), dma((n_head - 1,)),
         ],
         compiler_params=pltpu.CompilerParams(
-            collective_id=0, has_side_effects=True, vmem_limit_bytes=32 * 1024 * 1024
+            collective_id=0, has_side_effects=True, vmem_limit_bytes=64 * 1024 * 1024
         ),
     )(decay_rate, doc_lengths, queries, key_rows, value_rows, carry_state, norm_gain.reshape(1, features), order)
 

time: 29 us -> 24.2 us (0.83); the launches traced: 28.5 us -> 24 us
  local copies, waits for them, and re-layouts: 6.52 us -> 1.67 us
  Pallas kernels: 21.9 us -> 22.3 us
    unnamed x17 -> x1, local copies, waits for them, and re-layouts: 6.52 us -> 1.67 us
    pallas_call x1, Pallas kernels: 21.9 us -> 22.3 us  [shards(): pl.pallas_call(functools.partial(kernel, n_ctx, n_head, reach), out_shape...]
where the time goes in v2:
time: 24.2 us; the launch traced here: 24 us
  Pallas kernels  22.3 us (92%)
  local copies, waits for them, and re-layouts  1.67 us (7%)
    pallas_call x1, Pallas kernels, shards(): pl.pallas_call(functools.partial(kernel, n_ctx, n_head, reach), out_shape...  22.3 us
    unnamed x1, local copies, waits for them, and re-layouts  1.67 us

profile of v2, /device:TPU:0, one launch (start us, length us, event | category | flops | bytes accessed | tf_op | source)
XLA Modules:
  0.0 24.0 jit_solution(17761624222310394533)
XLA Ops:
  0.0 22.3 %shard_map.82 = bf16[256,512]{1,0:T(8,128)(2,1)} custom-call(f32[4]{0:T(128)} %rate_hbm.1, s32[16]{0:T(128)} %docs_hbm.1, bf16[256,512]{1,0:T(8,128)(2,1)} %q_hbm.1, bf16[256,512]{1,0:T(8,128)(2,1)} %k_hbm.1, bf16[256,512]{1,0:T(8,128)(2,1)} %v_hbm.1, f32[4,128,128]{2,1,0:T(8,128)} %carry_hbm.1, f32[1,512]{1,0:T(1,128)} %bitcast.1, s32[1,256]{1,0:T(1,128)} %order_hbm.1), custom_call_target="tpu_custom_call" | custom-call | tf_op jit(solution)/shard_map/pallas_call | solution.py:260
  22.3 1.7 %copy.10 = bf16[256,512]{1,0:T(8,128)(2,1)} copy(bf16[256,512]{1,0:T(8,128)(2,1)} %shard_map.82) | data formatting | bytes 524288

commit v3 on v2

--- a/solution.py
+++ b/solution.py
@@ -27,11 +27,25 @@
     return both[:, :width] + both[:, width:]
 
 
+def coded(x):
+    top = jnp.maximum(jnp.max(jnp.abs(x), axis=0, keepdims=True), 1e-30)
+    level = jnp.ceil(jnp.log2(top) * 16.0)
+    counts = jnp.round(x * (jnp.exp2(level * -0.0625) * 32760.0))
+    rows = jnp.concatenate([counts, jnp.broadcast_to(level, (16, x.shape[1]))], axis=0)
+    return rows.astype(jnp.int32).astype(jnp.int16)
+
+
+def decoded(ref, index):
+    whole = ref[index].astype(jnp.int32).astype(F32)
+    width = whole.shape[1]
+    return whole[:width] * (jnp.exp2(whole[width : width + 1] * 0.0625) * (1.0 / 32760.0))
+
+
 def kernel(
     n_ctx, n_head, reach,
     rate_hbm, docs_hbm, q_hbm, k_hbm, v_hbm, carry_hbm, gain_hbm, order_hbm, out_ref,
     rate_ref, docs_ref, q_ref, k_ref, v_ref, carry_ref, gain_ref, order_ref, load_sem,
-    attn, pair, away, layer, landed, onward, arrived, squares, squares_in,
+    attn, pair, pair_in, away, layer, landed, entering, onward, arrived, squares, squares_in,
     pair_send, pair_recv, layer_send, layer_recv, onward_send, onward_recv, sq_send, sq_recv,
 ):
     rows, features = q_ref.shape
@@ -103,21 +117,26 @@
     pair_base = jnp.where(u == 0, tokens, 2 * u * rows) - spill
     marks = (last, pair_last, first_last, pair_base - 1)
 
-    def document(n, carried):
-        edge, begin, scalars = carried
+    def over_documents(step, state):
+        if n_docs <= 32:
+            for n in range(n_docs):
+                state = step(n, state)
+            return state
+        return lax.fori_loop(0, n_docs, step, state)
+
+    def scalar_starts(n, carried):
+        edge, starts = carried
+        edge = edge + docs_ref[n]
+        return edge, tuple(jnp.where(m >= edge, edge, s) for m, s in zip(marks, starts))
+
+    def row_starts(n, carried):
+        edge, begin = carried
         edge = edge + docs_ref[n]
         mark = edge.astype(F32)
-        begin = jnp.where(pos >= mark, mark, begin)
-        return edge, begin, tuple(jnp.where(m >= edge, edge, s) for m, s in zip(marks, scalars))
+        return edge, jnp.where(pos >= mark, mark, begin)
 
     zero = jnp.int32(0)
-    state = (zero, jnp.zeros((rows, width), F32), (zero,) * 4)
-    if n_docs <= 32:
-        for n in range(n_docs):
-            state = document(n, state)
-    else:
-        state = lax.fori_loop(0, n_docs, document, state)
-    _, begin, (last_begin, pair_begin, first_begin, base_begin) = state
+    last_begin, pair_begin, first_begin, base_begin = over_documents(scalar_starts, (zero, (zero,) * 4))[1]
 
     inf = jnp.float32(jnp.inf)
 
@@ -146,34 +165,25 @@
 
     pair_copies = []
     for i in range(half):
-        away[i] = own_state(other + i)
+        away[i] = coded(own_state(other + i))
         if i == 0:
             pl.semaphore_wait(barrier, expected)
-        c = copy(away.at[i], pair.at[y, i], pair_send.at[i], pair_recv.at[i], (partner, g))
+        c = copy(away.at[i], pair_in.at[i], pair_send.at[i], pair_recv.at[i], (partner, g))
         c.start()
         pair_copies.append(c)
     for i in range(half):
-        pair[y, i] = own_state(mine + i)
-
-    def layer_copy(b, i):
-        target = lax.rem(u + b, n_pairs) * 2 + y
-        return copy(layer.at[i], landed.at[b - 1, i], layer_send.at[b - 1, i], layer_recv.at[b - 1, i], (target, g))
-
-    for i in range(half):
-        pair_copies[i].wait_recv()
-        layer[i] = pair[1, i] + factor(mine + i, rows, pair_begin <= pair_last - rows) * pair[0, i]
-        for b in range(1, reach + 1):
-            @pl.when(sends(b))
-            def _():
-                layer_copy(b, i).start()
-
+        pair[i] = own_state(mine + i)
+
+    begin = over_documents(row_starts, (zero, jnp.zeros((rows, width), F32)))[1]
     gap = down - across
     begins = jnp.concatenate([begin] * (rows // width), axis=1)
     gap = jnp.where((gap >= 0) & (across >= begins), gap, inf)
     to_carry = jnp.where(begin == 0, pos + 1, inf)
-    loads[id(q_ref)].wait()
-    loads[id(carry_ref)].wait()
-    for h in range(heads):
+    to_base = jnp.where(
+        (pos >= base.astype(F32)) & (begin < base.astype(F32)), pos - (base - 1).astype(F32), inf
+    )
+
+    def add_local(h):
         cols = slice(h * width, (h + 1) * width)
         q, v = q_ref[:, cols], v_ref[:, cols]
         weights = dot(q, k_ref[:, cols], (1, 1)) * decay(h, gap)
@@ -181,13 +191,30 @@
         local = dot(high, v, (1, 0)) + dot(low, v, (1, 0))
         attn[:, cols] = local + two_term(q, carry_ref[h], (1, 0)) * decay(h, to_carry)
 
-    to_base = jnp.where(
-        (pos >= base.astype(F32)) & (begin < base.astype(F32)), pos - (base - 1).astype(F32), inf
-    )
+    loads[id(q_ref)].wait()
+    loads[id(carry_ref)].wait()
+
+    def layer_copy(b, i):
+        target = lax.rem(u + b, n_pairs) * 2 + y
+        return copy(layer.at[i], landed.at[b - 1, i], layer_send.at[b - 1, i], layer_recv.at[b - 1, i], (target, g))
+
+    is_first = y == 0
+    for i in range(half):
+        pair_copies[i].wait_recv()
+        theirs, ours = decoded(pair_in, i), pair[i]
+        first = jnp.where(is_first, ours, theirs)
+        second = jnp.where(is_first, theirs, ours)
+        layer[i] = coded(second + factor(mine + i, rows, pair_begin <= pair_last - rows) * first)
+        pair[i] = first
+        for b in range(1, reach + 1):
+            @pl.when(sends(b))
+            def _():
+                layer_copy(b, i).start()
+    for h in range(heads):
+        add_local(h)
 
     def add_incoming(h, incoming):
-        entering = two_term(columns(q_ref, h), incoming, (1, 0)) * decay(h, to_base)
-        total = columns(attn, h) + entering
+        total = columns(attn, h) + two_term(columns(q_ref, h), incoming, (1, 0)) * decay(h, to_base)
         attn[:, pl.ds(pl.multiple_of(h * width, width), width)] = total
         return total * total
 
@@ -195,17 +222,17 @@
     kept = []
     for i in range(half):
         h = mine + i
-        onward[i] = jnp.zeros((width, width), F32)
+        entering[i] = jnp.zeros((width, width), F32)
         for b in range(1, reach + 1):
             @pl.when(receives(b))
             def _():
                 layer_copy(b, i).wait_recv()
                 steps = 2 * rows * (b - 1)
-                onward[i] += factor(h, steps, base_begin <= pair_base - 1 - steps) * landed[b - 1, i]
-        before_first = onward[i]
-        before_second = pair[0, i] + factor(h, rows, first_begin <= first_last - rows) * before_first
-        is_first = y == 0
-        onward[i] = jnp.where(is_first, before_second, before_first)
+                fade = factor(h, steps, base_begin <= pair_base - 1 - steps)
+                entering[i] += fade * decoded(landed, (b - 1, i))
+        before_first = entering[i]
+        before_second = pair[i] + factor(h, rows, first_begin <= first_last - rows) * before_first
+        onward[i] = coded(jnp.where(is_first, before_second, before_first))
         c = copy(onward.at[i], arrived.at[i], onward_send.at[i], onward_recv.at[i], (partner, g))
         c.start()
         onward_copies.append(c)
@@ -215,7 +242,7 @@
         power += add_incoming(mine + i, kept[i])
     for i in range(half):
         onward_copies[i].wait_recv()
-        power += add_incoming(other + i, arrived[i])
+        power += add_incoming(other + i, decoded(arrived, i))
 
     ones = jnp.ones((16, width), BF16)
     high, low = split(power)
@@ -273,12 +300,14 @@
             pltpu.VMEM(order.shape, jnp.int32),
             dma((8,)),
             pltpu.VMEM((rows, features), F32),
-            pltpu.VMEM((2, half, width, width), F32),
             pltpu.VMEM((half, width, width), F32),
+            pltpu.VMEM((half, width + 16, width), jnp.int16),
+            pltpu.VMEM((half, width + 16, width), jnp.int16),
+            pltpu.VMEM((half, width + 16, width), jnp.int16),
+            pltpu.VMEM((reach, half, width + 16, width), jnp.int16),
             pltpu.VMEM((half, width, width), F32),
-            pltpu.VMEM((reach, half, width, width), F32),
-            pltpu.VMEM((half, width, width), F32),
-            pltpu.VMEM((half, width, width), F32),
+            pltpu.VMEM((half, width + 16, width), jnp.int16),
+            pltpu.VMEM((half, width + 16, width), jnp.int16),
             pltpu.VMEM((8, rows), F32),
             pltpu.VMEM((n_head - 1, 8, rows), F32),
             dma((half,)), dma((half,)),

time: 24.2 us -> 21.4 us (0.88)
  Pallas kernels: 22.3 us -> 19.6 us
    pallas_call x1, Pallas kernels: 22.3 us -> 19.6 us  [shards(): pl.pallas_call(functools.partial(kernel, n_ctx, n_head, reach), out_shape...]
where the time goes in v3:
time: 21.4 us; the launch traced here: 21.2 us
  Pallas kernels  19.6 us (92%)
  local copies, waits for them, and re-layouts  1.67 us (8%)
    pallas_call x1, Pallas kernels, shards(): pl.pallas_call(functools.partial(kernel, n_ctx, n_head, reach), out_shape...  19.6 us
    unnamed x1, local copies, waits for them, and re-layouts  1.67 us

profile of v3, /device:TPU:0, one launch (start us, length us, event | category | flops | bytes accessed | tf_op | source)
XLA Modules:
  0.0 21.2 jit_solution(5385839745123722243)
XLA Ops:
  0.0 19.6 %shard_map.82 = bf16[256,512]{1,0:T(8,128)(2,1)} custom-call(f32[4]{0:T(128)} %rate_hbm.1, s32[16]{0:T(128)} %docs_hbm.1, bf16[256,512]{1,0:T(8,128)(2,1)} %q_hbm.1, bf16[256,512]{1,0:T(8,128)(2,1)} %k_hbm.1, bf16[256,512]{1,0:T(8,128)(2,1)} %v_hbm.1, f32[4,128,128]{2,1,0:T(8,128)} %carry_hbm.1, f32[1,512]{1,0:T(1,128)} %bitcast.1, s32[1,256]{1,0:T(1,128)} %order_hbm.1), custom_call_target="tpu_custom_call" | custom-call | tf_op jit(solution)/shard_map/pallas_call | solution.py:287
  19.6 1.7 %copy.10 = bf16[256,512]{1,0:T(8,128)(2,1)} copy(bf16[256,512]{1,0:T(8,128)(2,1)} %shard_map.82) | data formatting | bytes 524288

commit v4 on v3

--- a/solution.py
+++ b/solution.py
@@ -46,7 +46,7 @@
     rate_hbm, docs_hbm, q_hbm, k_hbm, v_hbm, carry_hbm, gain_hbm, order_hbm, out_ref,
     rate_ref, docs_ref, q_ref, k_ref, v_ref, carry_ref, gain_ref, order_ref, load_sem,
     attn, pair, pair_in, away, layer, landed, entering, onward, arrived, squares, squares_in,
-    pair_send, pair_recv, layer_send, layer_recv, onward_send, onward_recv, sq_send, sq_recv,
+    pair_send, pair_recv, layer_send, layer_recv, wrap_send, onward_send, onward_recv, sq_send, sq_recv,
 ):
     rows, features = q_ref.shape
     heads = rate_ref.shape[0]
@@ -65,8 +65,13 @@
     mine = y * half
     other = (1 - y) * half
 
-    def sends(b):
-        return u + b <= n_pairs
+    inner = u + 1 < n_pairs
+
+    def forwards(b):
+        return inner & (u >= b - 1)
+
+    def wraps(b):
+        return u == n_pairs - b
 
     def receives(b):
         return (u >= b) | (u == 0)
@@ -86,13 +91,16 @@
         pl.semaphore_signal(
             barrier, inc=1, device_id=(d, lax.rem(g + n_head - j, n_head)), device_id_type=MESH
         )
-    expected = jnp.int32(n_head)
+
+    @pl.when(u > 0)
+    def _():
+        pl.semaphore_signal(barrier, inc=1, device_id=(d - 2, g), device_id_type=MESH)
+    expected = n_head + inner.astype(jnp.int32)
     for b in range(1, reach + 1):
-        @pl.when(receives(b))
+        @pl.when(u == 0)
         def _():
-            source = lax.rem(u + n_pairs - b, n_pairs) * 2 + y
-            pl.semaphore_signal(barrier, inc=1, device_id=(source, g), device_id_type=MESH)
-        expected = expected + sends(b).astype(jnp.int32)
+            pl.semaphore_signal(barrier, inc=1, device_id=(2 * (n_pairs - b) + y, g), device_id_type=MESH)
+        expected = expected + wraps(b).astype(jnp.int32)
 
     for held in (order_ref, docs_ref, rate_ref):
         loads[id(held)].wait()
@@ -194,9 +202,22 @@
     loads[id(q_ref)].wait()
     loads[id(carry_ref)].wait()
 
-    def layer_copy(b, i):
-        target = lax.rem(u + b, n_pairs) * 2 + y
-        return copy(layer.at[i], landed.at[b - 1, i], layer_send.at[b - 1, i], layer_recv.at[b - 1, i], (target, g))
+    def forward_copy(b, i):
+        source = layer.at[i] if b == 1 else landed.at[b - 2, i]
+        target = lax.rem(d + 2, n_ctx)
+        return copy(source, landed.at[b - 1, i], layer_send.at[b - 1, i], layer_recv.at[b - 1, i], (target, g))
+
+    def wrap_copy(b, i):
+        return copy(layer.at[i], landed.at[b - 1, i], wrap_send.at[i], layer_recv.at[b - 1, i], (y, g))
+
+    def forward(b, i):
+        @pl.when(u >= b - 1)
+        def _():
+            forward_copy(b - 1, i).wait_recv()
+
+        @pl.when(forwards(b))
+        def _():
+            forward_copy(b, i).start()
 
     is_first = y == 0
     for i in range(half):
@@ -206,12 +227,20 @@
         second = jnp.where(is_first, theirs, ours)
         layer[i] = coded(second + factor(mine + i, rows, pair_begin <= pair_last - rows) * first)
         pair[i] = first
+        @pl.when(forwards(1))
+        def _():
+            forward_copy(1, i).start()
         for b in range(1, reach + 1):
-            @pl.when(sends(b))
+            @pl.when(wraps(b))
             def _():
-                layer_copy(b, i).start()
+                wrap_copy(b, i).start()
+    hops = [(b, i) for b in range(2, reach + 1) for i in range(half)]
     for h in range(heads):
         add_local(h)
+        if h >= 1 and hops:
+            forward(*hops.pop(0))
+    for hop in hops:
+        forward(*hop)
 
     def add_incoming(h, incoming):
         total = columns(attn, h) + two_term(columns(q_ref, h), incoming, (1, 0)) * decay(h, to_base)
@@ -226,7 +255,10 @@
         for b in range(1, reach + 1):
             @pl.when(receives(b))
             def _():
-                layer_copy(b, i).wait_recv()
+                @pl.when((u == 0) | (b == reach))
+                def _():
+                    forward_copy(b, i).wait_recv()
+
                 steps = 2 * rows * (b - 1)
                 fade = factor(h, steps, base_begin <= pair_base - 1 - steps)
                 entering[i] += fade * decoded(landed, (b - 1, i))
@@ -269,9 +301,13 @@
         c.wait_send()
     for i in range(half):
         for b in range(1, reach + 1):
-            @pl.when(sends(b))
+            @pl.when(forwards(b))
             def _():
-                layer_copy(b, i).wait_send()
+                forward_copy(b, i).wait_send()
+
+            @pl.when(wraps(b))
+            def _():
+                wrap_copy(b, i).wait_send()
 
 
 def shards(queries, key_rows, value_rows, carry_state, decay_rate, norm_gain, order, doc_lengths):
@@ -311,7 +347,7 @@
             pltpu.VMEM((8, rows), F32),
             pltpu.VMEM((n_head - 1, 8, rows), F32),
             dma((half,)), dma((half,)),
-            dma((reach, half)), dma((reach, half)),
+            dma((reach, half)), dma((reach, half)), dma((half,)),
             dma((half,)), dma((half,)),
             dma((n_head - 1,)), dma((n_head - 1,)),
         ],

time: 21.4 us -> 21.4 us (level)
  no operation moved by 1% of the time
where the time goes in v4:
time: 21.4 us; the launch traced here: 21.3 us
  Pallas kernels  19.6 us (92%)
  local copies, waits for them, and re-layouts  1.67 us (8%)
    pallas_call x1, Pallas kernels, shards(): pl.pallas_call(functools.partial(kernel, n_ctx, n_head, reach), out_shape...  19.6 us
    unnamed x1, local copies, waits for them, and re-layouts  1.67 us

profile of v4, /device:TPU:0, one launch (start us, length us, event | category | flops | bytes accessed | tf_op | source)
XLA Modules:
  0.0 21.3 jit_solution(9658872114147739086)
XLA Ops:
  0.0 19.6 %shard_map.82 = bf16[256,512]{1,0:T(8,128)(2,1)} custom-call(f32[4]{0:T(128)} %rate_hbm.1, s32[16]{0:T(128)} %docs_hbm.1, bf16[256,512]{1,0:T(8,128)(2,1)} %q_hbm.1, bf16[256,512]{1,0:T(8,128)(2,1)} %k_hbm.1, bf16[256,512]{1,0:T(8,128)(2,1)} %v_hbm.1, f32[4,128,128]{2,1,0:T(8,128)} %carry_hbm.1, f32[1,512]{1,0:T(1,128)} %bitcast.1, s32[1,256]{1,0:T(1,128)} %order_hbm.1), custom_call_target="tpu_custom_call" | custom-call | tf_op jit(solution)/shard_map/pallas_call | solution.py:323
  19.6 1.7 %copy.10 = bf16[256,512]{1,0:T(8,128)(2,1)} copy(bf16[256,512]{1,0:T(8,128)(2,1)} %shard_map.82) | data formatting | bytes 524288

commit v5 on v4

--- a/solution.py
+++ b/solution.py
@@ -43,8 +43,8 @@
 
 def kernel(
     n_ctx, n_head, reach,
-    rate_hbm, docs_hbm, q_hbm, k_hbm, v_hbm, carry_hbm, gain_hbm, order_hbm, out_ref,
-    rate_ref, docs_ref, q_ref, k_ref, v_ref, carry_ref, gain_ref, order_ref, load_sem,
+    rate_hbm, docs_hbm, q_hbm, k_hbm, v_hbm, carry_hbm, gain_hbm, order_hbm, out_hbm,
+    rate_ref, docs_ref, q_ref, k_ref, v_ref, carry_ref, gain_ref, order_ref, load_sem, out_ref, store_sem,
     attn, pair, pair_in, away, layer, landed, entering, onward, arrived, squares, squares_in,
     pair_send, pair_recv, layer_send, layer_recv, wrap_send, onward_send, onward_recv, sq_send, sq_recv,
 ):
@@ -83,7 +83,8 @@
     )
     for n, (source, held) in enumerate(operands):
         loads[id(held)] = pltpu.make_async_copy(source, held, load_sem.at[n])
-        loads[id(held)].start()
+        if n < 5:
+            loads[id(held)].start()
 
     barrier = pltpu.get_barrier_semaphore()
     pl.semaphore_signal(barrier, inc=1, device_id=(partner, g), device_id_type=MESH)
@@ -102,6 +103,8 @@
             pl.semaphore_signal(barrier, inc=1, device_id=(2 * (n_pairs - b) + y, g), device_id_type=MESH)
         expected = expected + wraps(b).astype(jnp.int32)
 
+    for held in (q_ref, carry_ref, gain_ref):
+        loads[id(held)].start()
     for held in (order_ref, docs_ref, rate_ref):
         loads[id(held)].wait()
 
@@ -293,10 +296,18 @@
     scale = lax.rsqrt(total / jnp.float32(features * n_head) + 1e-5)
     scale = jnp.broadcast_to(scale[0:1], (width, rows)).T
     loads[id(gain_ref)].wait()
+
+    def store(h):
+        cols = slice(h * width, (h + 1) * width)
+        return pltpu.make_async_copy(out_ref.at[:, cols], out_hbm.at[:, cols], store_sem.at[h])
+
     for h in range(heads):
         cols = slice(h * width, (h + 1) * width)
         out_ref[:, cols] = (attn[:, cols] * scale * gain_ref[:, cols]).astype(BF16)
-
+        store(h).start()
+
+    for h in range(heads):
+        store(h).wait()
     for c in pair_copies + onward_copies + sq_copies:
         c.wait_send()
     for i in range(half):
@@ -308,6 +319,18 @@
             @pl.when(wraps(b))
             def _():
                 wrap_copy(b, i).wait_send()
+
+
+def hand_over(parts, source, out, sem):
+    size = source.shape[0] // parts
+    copies = [
+        pltpu.make_async_copy(source.at[pl.ds(n * size, size)], out.at[pl.ds(n * size, size)], sem.at[n])
+        for n in range(parts)
+    ]
+    for c in copies:
+        c.start()
+    for c in copies:
+        c.wait()
 
 
 def shards(queries, key_rows, value_rows, carry_state, decay_rate, norm_gain, order, doc_lengths):
@@ -317,14 +340,13 @@
     longest = min(n_ctx * rows // 2, 2048)
     reach = -(-longest // (2 * rows))
     half = heads // 2
-    vmem = pl.BlockSpec(memory_space=pltpu.VMEM)
     hbm = pl.BlockSpec(memory_space=pltpu.HBM)
     dma = pltpu.SemaphoreType.DMA
-    return pl.pallas_call(
+    result = pl.pallas_call(
         functools.partial(kernel, n_ctx, n_head, reach),
         out_shape=jax.ShapeDtypeStruct((rows, features), BF16),
         in_specs=[hbm] * 8,
-        out_specs=vmem,
+        out_specs=hbm,
         scratch_shapes=[
             pltpu.SMEM(decay_rate.shape, F32),
             pltpu.SMEM(doc_lengths.shape, jnp.int32),
@@ -335,6 +357,8 @@
             pltpu.VMEM((1, features), F32),
             pltpu.VMEM(order.shape, jnp.int32),
             dma((8,)),
+            pltpu.VMEM((rows, features), BF16),
+            dma((heads,)),
             pltpu.VMEM((rows, features), F32),
             pltpu.VMEM((half, width, width), F32),
             pltpu.VMEM((half, width + 16, width), jnp.int16),
@@ -355,6 +379,15 @@
             collective_id=0, has_side_effects=True, vmem_limit_bytes=64 * 1024 * 1024
         ),
     )(decay_rate, doc_lengths, queries, key_rows, value_rows, carry_state, norm_gain.reshape(1, features), order)
+    parts = 8
+    return pl.pallas_call(
+        functools.partial(hand_over, parts),
+        out_shape=jax.ShapeDtypeStruct((rows, features), BF16),
+        in_specs=[hbm],
+        out_specs=hbm,
+        scratch_shapes=[dma((parts,))],
+        compiler_params=pltpu.CompilerParams(vmem_limit_bytes=64 * 1024 * 1024),
+    )(result)
 
 
 def solution(mesh):

time: 21.4 us -> 28.9 us (1.35)
  Pallas kernels: 19.6 us -> 28.7 us
  local copies, waits for them, and re-layouts: 1.67 us -> 0 us
    pallas_call x0 -> x1, Pallas kernels: none -> 9.12 us  [shards(): pl.pallas_call(functools.partial(hand_over, parts), out_shape=jax.ShapeDt...]
    unnamed x1 -> x0, local copies, waits for them, and re-layouts: 1.67 us -> none
where the time goes in v5:
time: 28.9 us; the launch traced here: 28.7 us
  Pallas kernels  28.7 us (99%)
    pallas_call x1, Pallas kernels, shards(): pl.pallas_call(functools.partial(kernel, n_ctx, n_head, reach), out_shape...  19.6 us
    pallas_call x1, Pallas kernels, shards(): pl.pallas_call(functools.partial(hand_over, parts), out_shape=jax.ShapeDt...  9.12 us

profile of v5, /device:TPU:0, one launch (start us, length us, event | category | flops | bytes accessed | tf_op | source)
XLA Modules:
  0.0 28.7 jit_solution(6543470452157121386)
XLA Ops:
  0.0 19.6 %shard_map.82.source = bf16[256,512]{1,0:T(8,128)(2,1)} custom-call(f32[4]{0:T(128)} %rate_hbm.1, s32[16]{0:T(128)} %docs_hbm.1, bf16[256,512]{1,0:T(8,128)(2,1)} %q_hbm.1, bf16[256,512]{1,0:T(8,128)(2,1)} %k_hbm.1, bf16[256,512]{1,0:T(8,128)(2,1)} %v_hbm.1, f32[4,128,128]{2,1,0:T(8,128)} %carry_hbm.1, f32[1,512]{1,0:T(1,128)} %bitcast.1, s32[1,256]{1,0:T(1,128)} %order_hbm.1), custom_call_target="tpu_custom_call" | custom-call | tf_op jit(solution)/shard_map/pallas_call | solution.py:345
  19.6 9.1 %shard_map.83 = bf16[256,512]{1,0:T(8,128)(2,1)} custom-call(bf16[256,512]{1,0:T(8,128)(2,1)} %shard_map.82.source), custom_call_target="tpu_custom_call" | custom-call | tf_op jit(solution)/shard_map/pallas_call | solution.py:383

commit v6 on v4

--- a/solution.py
+++ b/solution.py
@@ -43,8 +43,8 @@
 
 def kernel(
     n_ctx, n_head, reach,
-    rate_hbm, docs_hbm, q_hbm, k_hbm, v_hbm, carry_hbm, gain_hbm, order_hbm, out_ref,
-    rate_ref, docs_ref, q_ref, k_ref, v_ref, carry_ref, gain_ref, order_ref, load_sem,
+    rate_hbm, docs_hbm, q_hbm, k_hbm, v_hbm, carry_hbm, order_hbm, out_ref,
+    rate_ref, docs_ref, q_ref, k_ref, v_ref, carry_ref, order_ref, load_sem,
     attn, pair, pair_in, away, layer, landed, entering, onward, arrived, squares, squares_in,
     pair_send, pair_recv, layer_send, layer_recv, wrap_send, onward_send, onward_recv, sq_send, sq_recv,
 ):
@@ -79,7 +79,7 @@
     loads = {}
     operands = (
         (order_hbm, order_ref), (docs_hbm, docs_ref), (rate_hbm, rate_ref), (v_hbm, v_ref),
-        (k_hbm, k_ref), (q_hbm, q_ref), (carry_hbm, carry_ref), (gain_hbm, gain_ref),
+        (k_hbm, k_ref), (q_hbm, q_ref), (carry_hbm, carry_ref),
     )
     for n, (source, held) in enumerate(operands):
         loads[id(held)] = pltpu.make_async_copy(source, held, load_sem.at[n])
@@ -292,10 +292,9 @@
         total = total + squares_in[j - 1]
     scale = lax.rsqrt(total / jnp.float32(features * n_head) + 1e-5)
     scale = jnp.broadcast_to(scale[0:1], (width, rows)).T
-    loads[id(gain_ref)].wait()
     for h in range(heads):
         cols = slice(h * width, (h + 1) * width)
-        out_ref[:, cols] = (attn[:, cols] * scale * gain_ref[:, cols]).astype(BF16)
+        out_ref[:, cols] = attn[:, cols] * scale
 
     for c in pair_copies + onward_copies + sq_copies:
         c.wait_send()
@@ -320,10 +319,10 @@
     vmem = pl.BlockSpec(memory_space=pltpu.VMEM)
     hbm = pl.BlockSpec(memory_space=pltpu.HBM)
     dma = pltpu.SemaphoreType.DMA
-    return pl.pallas_call(
+    scaled = pl.pallas_call(
         functools.partial(kernel, n_ctx, n_head, reach),
-        out_shape=jax.ShapeDtypeStruct((rows, features), BF16),
-        in_specs=[hbm] * 8,
+        out_shape=jax.ShapeDtypeStruct((rows, features), F32),
+        in_specs=[hbm] * 7,
         out_specs=vmem,
         scratch_shapes=[
             pltpu.SMEM(decay_rate.shape, F32),
@@ -332,9 +331,8 @@
             pltpu.VMEM((rows, features), BF16),
             pltpu.VMEM((rows, features), BF16),
             pltpu.VMEM(carry_state.shape, F32),
-            pltpu.VMEM((1, features), F32),
             pltpu.VMEM(order.shape, jnp.int32),
-            dma((8,)),
+            dma((7,)),
             pltpu.VMEM((rows, features), F32),
             pltpu.VMEM((half, width, width), F32),
             pltpu.VMEM((half, width + 16, width), jnp.int16),
@@ -354,7 +352,8 @@
         compiler_params=pltpu.CompilerParams(
             collective_id=0, has_side_effects=True, vmem_limit_bytes=64 * 1024 * 1024
         ),
-    )(decay_rate, doc_lengths, queries, key_rows, value_rows, carry_state, norm_gain.reshape(1, features), order)
+    )(decay_rate, doc_lengths, queries, key_rows, value_rows, carry_state, order)
+    return (scaled * norm_gain[None, :]).astype(BF16)
 
 
 def solution(mesh):

time: 21.4 us -> 21.5 us (level)
  other arithmetic: 0 us -> 1.79 us
  local copies, waits for them, and re-layouts: 1.67 us -> 0 us
    convert_element_type x0 -> x1, other arithmetic: none -> 1.79 us  [shards(): return (scaled * norm_gain[None, :]).astype(BF16)]
    unnamed x1 -> x0, local copies, waits for them, and re-layouts: 1.67 us -> none
where the time goes in v6:
time: 21.5 us; the launch traced here: 21.4 us
  Pallas kernels  19.6 us (91%)
  other arithmetic  1.79 us (8%)
    pallas_call x1, Pallas kernels, shards(): pl.pallas_call(functools.partial(kernel, n_ctx, n_head, reach), out_shape...  19.6 us
    convert_element_type x1, other arithmetic, shards(): return (scaled * norm_gain[None, :]).astype(BF16)  1.79 us

profile of v6, /device:TPU:0, one launch (start us, length us, event | category | flops | bytes accessed | tf_op | source)
XLA Modules:
  0.0 21.4 jit_solution(11910427990134359999)
XLA Ops:
  0.0 19.6 %shard_map.82 = f32[256,512]{1,0:T(8,128)} custom-call(f32[4]{0:T(128)} %rate_hbm.1, s32[16]{0:T(128)} %docs_hbm.1, bf16[256,512]{1,0:T(8,128)(2,1)} %q_hbm.1, bf16[256,512]{1,0:T(8,128)(2,1)} %k_hbm.1, bf16[256,512]{1,0:T(8,128)(2,1)} %v_hbm.1, f32[4,128,128]{2,1,0:T(8,128)} %carry_hbm.1, s32[1,256]{1,0:T(1,128)} %order_hbm.1), custom_call_target="tpu_custom_call" | custom-call | tf_op jit(solution)/shard_map/pallas_call | solution.py:322
  19.6 1.8 %multiply_convert_fusion = bf16[256,512]{1,0:T(8,128)(2,1)} fusion(f32[256,512]{1,0:T(8,128)} %shard_map.82, f32[512]{0:T(512)} %param.13), kind=kLoop, calls=%fused_computation | loop fusion | flops 262144 | bytes 788480 | tf_op jit(solution)/shard_map/convert_element_type | solution.py:356
